TPU v7x, 32 devices: a whole 2x2x4 slice. The times are simulated.
32 devices in a mesh: blk: 32 (over z, y, x, core).
Axes of the slice: x: 2, y: 2, z: 4, core: 2. Of those that a mesh axis runs over, the one named last changes fastest.
Arguments:
- rhs: float32 [32768, 256], P('blk'), may hold values from -6 to 6
- diag_inv: float32 [32768, 128], P('blk')
- factor_blocks: float32 [960, 128, 128], P('blk'), may hold values from -0.125 to 0.125
- order: int32 [256], P('blk'), may hold values from 0 to 7, as said below
- blk_row: int32 [960], P('blk'), may hold values from 0 to 255, as said below
- blk_col: int32 [960], P('blk'), may hold values from 0 to 255, as said below
Outputs:
- solution: float32 [32768, 256], P('blk')
Inputs may be any that keep to these rules, and one draw needn't show every extreme that they name: `order`: for each device d, entries d * 8 to d * 8 + 7 are a permutation of 0 to 7. `blk_row`: stored block j lies on device j // 30; with p = j % 30 and k = p // 10, its row is a block row of that same device whose level is above k. `blk_col`: with j, p and k as for blk_row and e = (p // 2) % 5, the 2 blocks that share j // 30, k and e have as columns, each once, the 2 block rows of level k of the device e places below j // 30, counted cyclically over all devices.
All inputs are finite; a program needn't handle non-finite values.
Results may differ from a plain program's by a relative error of at most 0.0001.
Values sent between devices are 32-bit elements; how exact they have to be, the bound alone decides.
A program may use at most 64 MiB of HBM per device.

v0:
```python
import functools

import jax
import jax.numpy as jnp
from jax import lax
from jax.experimental import pallas as pl
from jax.experimental.pallas import tpu as pltpu
from jax.sharding import PartitionSpec as P

LANES = 2
STEPS = 4
BAND = 4
PARTS = 2
GROUPS = BAND + 1
MESH = pl.DeviceIdType.MESH
F32 = jnp.float32
BF16 = jnp.bfloat16


def split(x):
    high = x.astype(BF16)
    return high, (x - high.astype(F32)).astype(BF16)


def dot(a, b):
    return jnp.dot(a, b, preferred_element_type=F32)


def kernel(
    n,
    order_ref,
    row_ref,
    col_ref,
    rhs_hbm,
    diag_hbm,
    factor_hbm,
    out_hbm,
    rhs_ref,
    diag_ref,
    factor_ref,
    diag_two,
    factor_two,
    where_to,
    acc,
    own,
    got,
    terms,
    load_sems,
    out_sems,
    send_sems,
    recv_sems,
):
    slots = order_ref.shape[0]
    size = diag_ref.shape[1]
    width = rhs_ref.shape[2] // PARTS
    me = lax.axis_index("blk")
    core = lax.rem(me, 2)
    chip = me // 2
    odd = lax.rem(chip, 2)
    partner = me + 1 - 2 * core
    buddy = me + 2 - 4 * odd
    above = lax.rem(me + 4, n)
    below = lax.rem(me + n - 4, n)

    loads = [
        pltpu.make_async_copy(src, dst, load_sems.at[at])
        for at, (src, dst) in enumerate(
            ((diag_hbm, diag_ref), (rhs_hbm, rhs_ref), (factor_hbm, factor_ref))
        )
    ]
    for load in loads:
        load.start()

    barrier = pltpu.get_barrier_semaphore()
    for device in (partner, buddy, below):
        pl.semaphore_signal(barrier, inc=1, device_id=(device,), device_id_type=MESH)
    pl.semaphore_wait(barrier, 3)

    slot_at = []
    for level in range(STEPS):
        one, two = order_ref[2 * level], order_ref[2 * level + 1]
        slot_at += [jnp.minimum(one, two), jnp.maximum(one, two)]

    def lane(m):
        return pl.ds(m * size, size)

    def own_at(level, part, m):
        return (part * STEPS + level) * LANES + m

    def copy(t, m, kind, src, entry, device):
        at = (t * LANES + m) * 4
        return pltpu.make_async_remote_copy(
            src_ref=src,
            dst_ref=got.at[t, entry - 1].at[lane(m)],
            send_sem=send_sems.at[at + kind],
            recv_sem=recv_sems.at[at + entry - 1],
            device_id=(device,),
            device_id_type=MESH,
        )

    def mine(t, m):
        return own.at[own_at(t // PARTS, lax.rem(t, PARTS), m)]

    def there(t, m, entry):
        return got.at[t, entry - 1].at[lane(m)]

    def send_own(t, m):
        copy(t, m, 0, mine(t, m), 4, above).start()

        @pl.when(odd == 0)
        def _():
            copy(t, m, 1, mine(t, m), 2, buddy).start()

        @pl.when(core == 0)
        def _():
            copy(t, m, 3, mine(t, m), 1, partner).start()

    def save(at):
        return pltpu.make_async_copy(own.at[at], out_hbm.at[at], out_sems.at[at])

    def take_far(t, m):
        copy(t, m, 0, mine(t, m), 4, above).wait_recv()

        @pl.when(odd == 1)
        def _():
            copy(t, m, 1, there(t, m, 4), 2, buddy).start()

        @pl.when(core == 1)
        def _():
            copy(t, m, 3, there(t, m, 4), 3, partner).start()

    def sent(t):
        for m in range(LANES):
            copy(t, m, 0, mine(t, m), 4, above).wait_send()

    def take_near(t, m):
        copy(t, m, 1, mine(t, m), 2, buddy).wait_recv()
        copy(t, m, 2, there(t, m, 2), 3 - 2 * core, partner).start()

    def take_other(t, m, entry):
        copy(t, m, 2, mine(t, m), entry, partner).wait_recv()

    def tall(x):
        return jnp.concatenate(split(x), axis=0)

    def multiply(two, x):
        every = dot(two, jnp.concatenate(split(x), axis=1))
        top = every[0:size, 0:width] + every[0:size, width:]
        return top + (every[size:, 0:width] + every[size:, width:])

    def solve(level, part, residual, send):
        t = level * PARTS + part
        for m in range(LANES):
            at = own_at(level, part, m)
            own[at] = multiply(diag_two[level * LANES + m], residual[m])
            send(t, m)
            save(at).start()

    def prepare(index, carry):
        c = lax.rem(index, LANES)
        base = index - c
        swapped = (col_ref[base] > col_ref[base + 1]).astype(jnp.int32)
        second = swapped + c - 2 * swapped * c
        factor_two[index] = tall(factor_ref[base + second])
        slot = row_ref[base] * (1 - second) + row_ref[base + 1] * second - me * slots
        position = jnp.int32(0)
        for p in range(slots):
            position = position + p * (slot_at[p] == slot).astype(jnp.int32)
        where_to[index] = position
        return carry

    def weight(j, position):
        return (where_to[j] == position).astype(jnp.int32).astype(F32)

    loads[0].wait()
    for p in range(slots):
        diag_two[p] = tall(diag_ref[slot_at[p]])
    loads[1].wait()

    def rhs_of(level, part):
        columns = slice(part * width, (part + 1) * width)
        return [rhs_ref[slot_at[level * LANES + m]][:, columns] for m in range(LANES)]

    solve(0, 0, rhs_of(0, 0), send_own)
    solve(0, 1, rhs_of(0, 1), lambda t, m: None)
    for level in range(1, STEPS):
        for part in range(PARTS):
            for m, block in enumerate(rhs_of(level, part)):
                acc[own_at(level, part, m)] = block
    loads[2].wait()
    lax.fori_loop(0, (STEPS - 1) * GROUPS * LANES, prepare, 0)
    sent(0)
    for m in range(LANES):
        send_own(1, m)

    def step(t, carry):
        k, part = t // PARTS, lax.rem(t, PARTS)
        ahead = k + 1
        first = k * GROUPS * LANES
        residual = [acc[own_at(ahead, part, m)] for m in range(LANES)]

        def use(entry, c, x):
            j = entry * LANES + c
            term = multiply(factor_two[first + j], x)
            terms[j] = term
            for m in range(LANES):
                residual[m] = residual[m] - weight(first + j, ahead * LANES + m) * term

        for m in range(LANES):
            take_far(t, m)
            take_near(t, m)
        for m in range(LANES):
            use(0, m, own[own_at(k, part, m)])
        for entry in (4, 2):
            for m in range(LANES):
                use(entry, m, got[t, entry - 1, lane(m), :])
        for m in range(LANES):
            for entry in (1, 3):
                take_other(t, m, entry)
        for m in range(LANES):
            for entry in (1, 3):
                use(entry, m, got[t, entry - 1, lane(m), :])

        def send(where, m):
            @pl.when(ahead < STEPS - 1)
            def _():
                if m == 0:
                    sent(where - 1)
                send_own(where, m)

        solve(ahead, part, residual, send)

        def later(level, inner):
            for m in range(LANES):
                total = acc[own_at(level, part, m)]
                for j in range(GROUPS * LANES):
                    total = total - weight(first + j, level * LANES + m) * terms[j]
                acc[own_at(level, part, m)] = total
            return inner

        lax.fori_loop(k + 2, STEPS, later, 0)
        return carry

    lax.fori_loop(0, (STEPS - 1) * PARTS, step, 0)

    sent((STEPS - 1) * PARTS - 1)

    def finish(t, carry):
        for m in range(LANES):
            for kind in range(1, 4):
                copy(t, m, kind, mine(t, m), 1, partner).wait_send()
        return carry

    lax.fori_loop(0, (STEPS - 1) * PARTS, finish, 0)
    for at in range(PARTS * slots):
        save(at).wait()


def arrange(order_ref, solved_ref, out_hbm, staged, sems):
    slots, _, columns = out_hbm.shape
    width = columns // PARTS
    slot_at = []
    for level in range(STEPS):
        one, two = order_ref[2 * level], order_ref[2 * level + 1]
        slot_at += [jnp.minimum(one, two), jnp.maximum(one, two)]
    copies = []
    for slot in range(slots):
        position = jnp.int32(0)
        for p in range(slots):
            position = position + p * (slot_at[p] == slot).astype(jnp.int32)
        position = jnp.minimum(position, slots - 1)
        for part in range(PARTS):
            columns_of = slice(part * width, (part + 1) * width)
            staged[slot, :, columns_of] = solved_ref[part * slots + position]
        copies.append(
            pltpu.make_async_copy(staged.at[slot], out_hbm.at[slot], sems.at[slot])
        )
        copies[-1].start()
    for copy in copies:
        copy.wait()


def body(rhs, diag_inv, factor_blocks, order, blk_row, blk_col):
    n = lax.axis_size("blk")
    rows, columns = rhs.shape
    size = diag_inv.shape[1]
    slots = order.shape[0]
    width = columns // PARTS
    two = LANES * size
    rounds = (STEPS - 1) * PARTS
    scratch = [
        pltpu.VMEM((slots, size, columns), F32),
        pltpu.VMEM((slots, size, size), F32),
        pltpu.VMEM(factor_blocks.shape, F32),
        pltpu.VMEM((slots, two, size), BF16),
        pltpu.VMEM((factor_blocks.shape[0], two, size), BF16),
        pltpu.SMEM((factor_blocks.shape[0],), jnp.int32),
        pltpu.VMEM((PARTS * slots, size, width), F32),
        pltpu.VMEM((PARTS * slots, size, width), F32),
        pltpu.VMEM((rounds, BAND, two, width), F32),
        pltpu.VMEM((GROUPS * LANES, size, width), F32),
        pltpu.SemaphoreType.DMA((3,)),
        pltpu.SemaphoreType.DMA((PARTS * slots,)),
        pltpu.SemaphoreType.DMA((rounds * LANES * 4,)),
        pltpu.SemaphoreType.DMA((rounds * LANES * 4,)),
    ]
    solved = pl.pallas_call(
        functools.partial(kernel, n),
        out_shape=jax.ShapeDtypeStruct((PARTS * slots, size, width), F32),
        in_specs=[pl.BlockSpec(memory_space=pltpu.SMEM)] * 3
        + [pl.BlockSpec(memory_space=pl.ANY)] * 3,
        out_specs=pl.BlockSpec(memory_space=pl.ANY),
        scratch_shapes=scratch,
        compiler_params=pltpu.CompilerParams(
            collective_id=0, has_side_effects=True, vmem_limit_bytes=56 * 1024 * 1024
        ),
        cost_estimate=pl.CostEstimate(
            flops=2 * 3 * (factor_blocks.shape[0] + slots) * size * size * columns,
            bytes_accessed=4 * (2 * rows * columns + rows * size + factor_blocks.size),
            transcendentals=0,
        ),
    )(
        order,
        blk_row,
        blk_col,
        rhs.reshape(slots, size, columns),
        diag_inv.reshape(slots, size, size),
        factor_blocks,
    )
    out = pl.pallas_call(
        arrange,
        out_shape=jax.ShapeDtypeStruct((slots, size, columns), F32),
        in_specs=[
            pl.BlockSpec(memory_space=pltpu.SMEM),
            pl.BlockSpec(memory_space=pltpu.VMEM),
        ],
        out_specs=pl.BlockSpec(memory_space=pl.ANY),
        scratch_shapes=[
            pltpu.VMEM((slots, size, columns), F32),
            pltpu.SemaphoreType.DMA((slots,)),
        ],
        cost_estimate=pl.CostEstimate(
            flops=0, bytes_accessed=8 * rows * columns, transcendentals=0
        ),
    )(order, solved)
    return out.reshape(rows, columns)


def solution(mesh):
    placed = (P("blk", None), P("blk", None), P("blk", None, None), P("blk"), P("blk"), P("blk"))
    return jax.shard_map(
        body, mesh=mesh, in_specs=placed, out_specs=P("blk", None), check_vma=False
    )
```

profile of v0, /device:TPU:1, one launch (start us, length us, event | category | flops | bytes accessed | tf_op | source)
XLA Modules:
  0.0 42.6 jit_solution(8091815315735586799)
XLA Ops:
  0.0 40.3 %shard_map.64.solved_ref = f32[16,128,128]{2,1,0:T(8,128)} custom-call(s32[8]{0:T(128)} %order_ref.3, s32[30]{0:T(128)} %row_ref.1, s32[30]{0:T(128)} %col_ref.1, f32[8,128,256]{2,1,0:T(8,128)} %bitcast.3, f32[8,128,128]{2,1,0:T(8,128)} %bitcast.4, f32[30,128,128]{2,1,0:T(8,128)} %factor_hbm.1), custom_call_target="tpu_custom_call" | custom-call | flops 956301312 | bytes 4587520 | tf_op jit(solution)/shard_map/pallas_call | solution.py:307
  40.4 2.3 %shard_map.65 = f32[8,128,256]{2,1,0:T(8,128)} custom-call(s32[8]{0:T(128)} %order_ref.3, f32[16,128,128]{2,1,0:T(8,128)} %shard_map.64.solved_ref), custom_call_target="tpu_custom_call" | custom-call | bytes 2097152 | tf_op jit(solution)/shard_map/pallas_call | solution.py:330
where the time goes:
time: 42.8 us; the launch traced here: 42.6 us
  Pallas kernels  42.6 us (100%)
    pallas_call x1, Pallas kernels, body(): pl.pallas_call(functools.partial(kernel, n), out_shape=jax.ShapeDtypeStru...  40.3 us
    pallas_call x1, Pallas kernels, body(): pl.pallas_call(arrange, out_shape=jax.ShapeDtypeStruct((slots, size, colu...  2.29 us

commit v1 on v0

--- a/solution.py
+++ b/solution.py
@@ -59,6 +59,7 @@
     odd = lax.rem(chip, 2)
     partner = me + 1 - 2 * core
     buddy = me + 2 - 4 * odd
+    following = lax.rem(me + 2, n)
     above = lax.rem(me + 4, n)
     below = lax.rem(me + n - 4, n)
 
@@ -74,7 +75,13 @@
     barrier = pltpu.get_barrier_semaphore()
     for device in (partner, buddy, below):
         pl.semaphore_signal(barrier, inc=1, device_id=(device,), device_id_type=MESH)
-    pl.semaphore_wait(barrier, 3)
+
+    @pl.when(odd == 0)
+    def _():
+        before = lax.rem(me + n - 2, n)
+        pl.semaphore_signal(barrier, inc=1, device_id=(before,), device_id_type=MESH)
+
+    pl.semaphore_wait(barrier, 3 + odd)
 
     slot_at = []
     for level in range(STEPS):
@@ -107,9 +114,14 @@
     def send_own(t, m):
         copy(t, m, 0, mine(t, m), 4, above).start()
 
-        @pl.when(odd == 0)
-        def _():
-            copy(t, m, 1, mine(t, m), 2, buddy).start()
+        if m == 0:
+
+            @pl.when(odd == 0)
+            def _():
+                copy(t, m, 1, mine(t, m), 2, buddy).start()
+
+        else:
+            copy(t, m, 1, mine(t, m), 2, following).start()
 
         @pl.when(core == 0)
         def _():
@@ -121,9 +133,11 @@
     def take_far(t, m):
         copy(t, m, 0, mine(t, m), 4, above).wait_recv()
 
-        @pl.when(odd == 1)
-        def _():
-            copy(t, m, 1, there(t, m, 4), 2, buddy).start()
+        if m == 0:
+
+            @pl.when(odd == 1)
+            def _():
+                copy(t, m, 1, there(t, m, 4), 2, buddy).start()
 
         @pl.when(core == 1)
         def _():
@@ -208,6 +222,7 @@
 
         for m in range(LANES):
             take_far(t, m)
+        for m in (1, 0):
             take_near(t, m)
         for m in range(LANES):
             use(0, m, own[own_at(k, part, m)])

time: 42.8 us -> 41.6 us (0.972)
  Pallas kernels: 42.6 us -> 41.4 us
    pallas_call x1, Pallas kernels: 40.3 us -> 39.1 us  [body(): pl.pallas_call(functools.partial(kernel, n), out_shape=jax.ShapeDtypeStru...]
where the time goes in v1:
time: 41.6 us; the launch traced here: 41.4 us
  Pallas kernels  41.4 us (100%)
    pallas_call x1, Pallas kernels, body(): pl.pallas_call(functools.partial(kernel, n), out_shape=jax.ShapeDtypeStru...  39.1 us
    pallas_call x1, Pallas kernels, body(): pl.pallas_call(arrange, out_shape=jax.ShapeDtypeStruct((slots, size, colu...  2.29 us

profile of v1, /device:TPU:1, one launch (start us, length us, event | category | flops | bytes accessed | tf_op | source)
XLA Modules:
  0.0 41.4 jit_solution(3405919732251140912)
XLA Ops:
  0.0 39.1 %shard_map.64.solved_ref = f32[16,128,128]{2,1,0:T(8,128)} custom-call(s32[8]{0:T(128)} %order_ref.3, s32[30]{0:T(128)} %row_ref.1, s32[30]{0:T(128)} %col_ref.1, f32[8,128,256]{2,1,0:T(8,128)} %bitcast.3, f32[8,128,128]{2,1,0:T(8,128)} %bitcast.4, f32[30,128,128]{2,1,0:T(8,128)} %factor_hbm.1), custom_call_target="tpu_custom_call" | custom-call | flops 956301312 | bytes 4587520 | tf_op jit(solution)/shard_map/pallas_call | solution.py:322
  39.2 2.3 %shard_map.65 = f32[8,128,256]{2,1,0:T(8,128)} custom-call(s32[8]{0:T(128)} %order_ref.3, f32[16,128,128]{2,1,0:T(8,128)} %shard_map.64.solved_ref), custom_call_target="tpu_custom_call" | custom-call | bytes 2097152 | tf_op jit(solution)/shard_map/pallas_call | solution.py:345
